TPU v7x, 512 devices: a whole 4x4x16 slice. The times are simulated.
512 devices in a mesh: diag: 32 (over x_lo, z), tile: 16 (over y, x_hi, core).
Axes of the slice: x: 4 (x_hi: 2, x_lo: 2; x = x_hi * 2 + x_lo), y: 4, z: 16, core: 2. Of those that a mesh axis runs over, the one named last changes fastest.
Arguments:
- tiles: bfloat16 [32, 16, 1280, 1280], P('diag', 'tile'), may hold values from -0.03125 to 0.03125
- live_groups: int32 [32, 16], P('diag', 'tile'), may hold values from 1 to 10, as said below
- vectors: bfloat16 [40960, 256], P('diag'), may hold values from -6 to 6
- previous: float32 [40960, 256], P('diag', 'tile'), may hold values from -6 to 6
- energies: float32 [40960], P('diag'), may hold values from 0.5 to 8
- beta_prev: float32 [256], P('tile'), may hold values from 0.3 to 1.5
Outputs:
- next_vector: float32 [40960, 256], P('diag', 'tile')
- alpha: float32 [256], P('tile')
- beta: float32 [256], P('tile')
Inputs may be any that keep to these rules, and one draw needn't show every extreme that they name: `live_groups`: every stored tile has at least one live group; in every draw some tile is fully live.
All inputs are finite; a program needn't handle non-finite values.
Results may differ from a plain program's by a relative error of at most 0.0015.
Values may be sent and summed in bfloat16 or wider, within the bound.
A program may use at most 64 MiB of HBM per device.

v0:
```python
import jax
import jax.numpy as jnp
from jax import lax
from jax.sharding import PartitionSpec as P

GROUP = 128


def from_behind(value, axis, steps):
    count = lax.axis_size(axis)
    pairs = [(source, (source + steps) % count) for source in range(count)]
    return lax.ppermute(value, axis, pairs)


def body(tiles, live_groups, vectors, previous, energies, beta_prev):
    tile_rows = tiles[0, 0]
    seg_rows = vectors.shape[0]
    columns = vectors.shape[1]
    offset = lax.axis_index("tile")
    groups = lax.axis_size("tile")
    share = columns // groups
    nbits = (groups - 1).bit_length()
    live = (jnp.arange(seg_rows, dtype=jnp.int32) < GROUP * live_groups[0, 0])[:, None]
    current = vectors
    for bit in range(nbits):
        moved = from_behind(current, "diag", 1 << bit)
        current = jnp.where(offset >> bit & 1 == 1, moved, current)
    direct = jnp.where(live, jnp.dot(tile_rows, current, preferred_element_type=jnp.float32), 0.0)
    masked = jnp.where(live, vectors, jnp.zeros_like(vectors))
    turned = lax.dot_general(
        tile_rows, masked, (((0,), (0,)), ((), ())), preferred_element_type=jnp.float32
    )
    for bit in range(nbits):
        moved_back = from_behind(turned.astype(jnp.bfloat16), "diag", -(1 << bit)).astype(
            turned.dtype
        )
        turned = jnp.where(offset >> bit & 1 == 1, moved_back, turned)
    local_terms = direct + turned
    summed = lax.psum(local_terms, "tile")
    row_part = lax.dynamic_slice_in_dim(summed, offset * share, share, 1)
    own = lax.dynamic_slice_in_dim(vectors, offset * share, share, 1).astype(jnp.float32)
    hv = row_part + energies[:, None] * own
    total_rows = seg_rows * lax.axis_size("diag")
    numer, denom = lax.psum((jnp.sum(own * hv, axis=0), jnp.sum(own * own, axis=0)), "diag")
    alpha = numer / denom
    resid = hv - alpha[None, :] * own - beta_prev[None, :] * previous
    squared = lax.psum(jnp.sum(resid * resid, axis=0), "diag")
    beta = jnp.sqrt(squared / total_rows + 1e-06)
    return (resid / beta[None, :], alpha, beta)


def solution(mesh):
    return jax.shard_map(
        body,
        mesh=mesh,
        in_specs=(
            P("diag", "tile", None, None),
            P("diag", "tile"),
            P("diag", None),
            P("diag", "tile"),
            P("diag"),
            P("tile"),
        ),
        out_specs=(P("diag", "tile"), P("tile"), P("tile")),
        check_vma=False,
    )
```

profile of v0, /device:TPU:32, one launch (start us, length us, event | category | flops | bytes accessed | tf_op | source)
XLA Modules:
  0.0 567.0 jit_solution(7222621045921417785)
XLA Ops:
  9.1 3.5 fusion.31
  12.6 7.4 %collective-permute-start.4 = (bf16[1280,256]{0,1:T(8,128)(2,1)}, bf16[1280,256]{0,1:T(8,128)(2,1)}, u32[]{:S(2)}, u32[]{:S(2)}) collective-permute-start(bf16[1280,256]{0,1:T(8,128)(2,1)} %get-tuple-element.11), channel_id=1, source_target_pairs={{0,496},{16,0},{32,16},{48,32},{64,48},{80,64},{96,80},{112,96},{1... | collective-permute-start | bytes 1966088 | tf_op jit(solution)/shard_map/ppermute | solution.py:12
  20.0 2.2 copy.9
  22.2 1.9 collective-permute-start
  24.1 7.4 %collective-permute-done.4 = bf16[1280,256]{0,1:T(8,128)(2,1)} collective-permute-done((bf16[1280,256]{0,1:T(8,128)(2,1)}, bf16[1280,256]{0,1:T(8,128)(2,1)}, u32[]{:S(2)}, u32[]{:S(2)}) %collective-permute-start.4) | collective-permute-done | bytes 655392 | tf_op jit(solution)/shard_map/ppermute | solution.py:12
  31.5 2.4 fusion.16
  33.9 13.8 %collective-permute-start.5 = (bf16[1280,256]{0,1:T(8,128)(2,1)}, bf16[1280,256]{0,1:T(8,128)(2,1)}, u32[]{:S(2)}, u32[]{:S(2)}) collective-permute-start(bf16[1280,256]{0,1:T(8,128)(2,1)} %fusion.16), channel_id=1, source_target_pairs={{0,480},{16,496},{32,0},{48,16},{64,32},{80,48},{96,64},{112,80},{... | collective-permute-start | bytes 1966088 | tf_op jit(solution)/shard_map/ppermute | solution.py:12
  47.7 1.3 broadcast_select_fusion
  49.0 1.9 collective-permute-start.1
  50.9 30.9 %collective-permute-done.5 = bf16[1280,256]{0,1:T(8,128)(2,1)} collective-permute-done((bf16[1280,256]{0,1:T(8,128)(2,1)}, bf16[1280,256]{0,1:T(8,128)(2,1)}, u32[]{:S(2)}, u32[]{:S(2)}) %collective-permute-start.5) | collective-permute-done | bytes 655392 | tf_op jit(solution)/shard_map/ppermute | solution.py:12
  81.8 2.8 fusion.30
  84.6 1.9 collective-permute-start.6
  87.5 7.8 %collective-permute-start.2 = (bf16[1280,256]{0,1:T(8,128)(2,1)}, bf16[1280,256]{0,1:T(8,128)(2,1)}, u32[]{:S(2)}, u32[]{:S(2)}) collective-permute-start(bf16[1280,256]{0,1:T(8,128)(2,1)} %broadcast_select_fusion.1), channel_id=1, source_target_pairs={{0,64},{16,80},{32,96},{48,112},{64,128},{80,144},{96,160},{112,17... | collective-permute-start | bytes 1966088 | tf_op jit(solution)/shard_map/ppermute | solution.py:12
  95.3 16.6 %collective-permute-done.6 = bf16[1280,256]{0,1:T(8,128)(2,1)} collective-permute-done((bf16[1280,256]{0,1:T(8,128)(2,1)}, bf16[1280,256]{0,1:T(8,128)(2,1)}, u32[]{:S(2)}, u32[]{:S(2)}) %collective-permute-start.6) | collective-permute-done | bytes 655392 | tf_op jit(solution)/shard_map/ppermute | solution.py:12
  111.9 2.5 fusion.17
  114.3 2.2 collective-permute-start.7
  116.5 47.3 %collective-permute-done.2 = bf16[1280,256]{0,1:T(8,128)(2,1)} collective-permute-done((bf16[1280,256]{0,1:T(8,128)(2,1)}, bf16[1280,256]{0,1:T(8,128)(2,1)}, u32[]{:S(2)}, u32[]{:S(2)}) %collective-permute-start.2) | collective-permute-done | bytes 655392 | tf_op jit(solution)/shard_map/ppermute | solution.py:12
  163.8 2.0 broadcast_select_fusion.2
  165.8 1.9 collective-permute-start.3
  167.8 47.9 %collective-permute-done.3 = bf16[1280,256]{0,1:T(8,128)(2,1)} collective-permute-done((bf16[1280,256]{0,1:T(8,128)(2,1)}, bf16[1280,256]{0,1:T(8,128)(2,1)}, u32[]{:S(2)}, u32[]{:S(2)}) %collective-permute-start.3) | collective-permute-done | bytes 655392 | tf_op jit(solution)/shard_map/ppermute | solution.py:12
  215.7 4.0 fusion.10
  219.8 213.1 %all-reduce.3.cloned.1.call-done = f32[1280,256]{0,1:T(8,128)} async-done(((f32[1280,256]{0,1:T(8,128)}), f32[1280,256]{0,1:T(8,128)}) %all-reduce.3.cloned.1.call-update) | async-done | bytes 1310736 | tf_op jit(solution)/shard_map/psum | solution.py:39
  433.9 61.7 %all-reduce = (f32[16]{0:T(128)S(1)}, f32[16]{0:T(128)S(1)}) all-reduce(f32[16]{0:T(128)S(1)} %get-tuple-element.4, f32[16]{0:T(128)S(1)} %get-tuple-element.3), channel_id=1, replica_groups=mesh['diag'=32,'tile'=16] {'diag'}, use_global_device_ids=true, to_apply=%region_2.3 | all-reduce | flops 32 | bytes 256 | tf_op jit(solution)/shard_map/psum | solution.py:44
  496.8 62.7 %psum.31 = f32[16]{0:T(128)S(1)} all-reduce(f32[16]{0:T(128)S(1)} %get-tuple-element.7), channel_id=1, replica_groups=mesh['diag'=32,'tile'=16] {'diag'}, use_global_device_ids=true, to_apply=%region_6.7 | all-reduce | flops 16 | bytes 128 | tf_op jit(solution)/shard_map/psum | solution.py:47
  (26 shorter events, 5.0 us)
Async XLA Ops:
  7.2 1.9 copy-start
  7.2 425.7 %all-reduce.3.cloned.1.call-start = ((), (), s32[]{:S(2)}) async-start(), calls=%async_computation | async-start | bytes 2621440 | tf_op jit(solution)/shard_map/psum | solution.py:39
  12.6 18.9 %collective-permute-start.4 = (bf16[1280,256]{0,1:T(8,128)(2,1)}, bf16[1280,256]{0,1:T(8,128)(2,1)}, u32[]{:S(2)}, u32[]{:S(2)}) collective-permute-start(bf16[1280,256]{0,1:T(8,128)(2,1)} %get-tuple-element.11), channel_id=1, source_target_pairs={{0,496},{16,0},{32,16},{48,32},{64,48},{80,64},{96,80},{112,96},{1... | collective-permute-start | bytes 1966088 | tf_op jit(solution)/shard_map/ppermute | solution.py:12
  22.2 25.5 %collective-permute-start = (bf16[1280,256]{0,1:T(8,128)(2,1)}, bf16[1280,256]{0,1:T(8,128)(2,1)}, u32[]{:S(2)}, u32[]{:S(2)}) collective-permute-start(bf16[1280,256]{0,1:T(8,128)(2,1)} %copy.9), channel_id=1, source_target_pairs={{0,16},{16,32},{32,48},{48,64},{64,80},{80,96},{96,112},{112,128},... | collective-permute-start | bytes 1966088 | tf_op jit(solution)/shard_map/ppermute | solution.py:12
  33.9 47.9 %collective-permute-start.5 = (bf16[1280,256]{0,1:T(8,128)(2,1)}, bf16[1280,256]{0,1:T(8,128)(2,1)}, u32[]{:S(2)}, u32[]{:S(2)}) collective-permute-start(bf16[1280,256]{0,1:T(8,128)(2,1)} %fusion.16), channel_id=1, source_target_pairs={{0,480},{16,496},{32,0},{48,16},{64,32},{80,48},{96,64},{112,80},{... | collective-permute-start | bytes 1966088 | tf_op jit(solution)/shard_map/ppermute | solution.py:12
  47.7 34.1 %copy-start.1 = (f32[1280,256]{0,1:T(8,128)S(1)}, f32[1280,256]{0,1:T(8,128)}, u32[]{:S(2)}) copy-start(f32[1280,256]{0,1:T(8,128)} %get-tuple-element.12) | copy-start | bytes 3932164
  49.0 37.5 %collective-permute-start.1 = (bf16[1280,256]{0,1:T(8,128)(2,1)S(1)}, bf16[1280,256]{0,1:T(8,128)(2,1)S(1)}, u32[]{:S(2)}, u32[]{:S(2)}) collective-permute-start(bf16[1280,256]{0,1:T(8,128)(2,1)S(1)} %broadcast_select_fusion), channel_id=1, source_target_pairs={{0,32},{16,48},{32,64},{48,80},{64,96},{80,112},{96,128},{112,144}... | collective-permute-start | bytes 1966088 | tf_op jit(solution)/shard_map/ppermute | solution.py:12
  84.6 27.3 %collective-permute-start.6 = (bf16[1280,256]{0,1:T(8,128)(2,1)}, bf16[1280,256]{0,1:T(8,128)(2,1)}, u32[]{:S(2)}, u32[]{:S(2)}) collective-permute-start(bf16[1280,256]{0,1:T(8,128)(2,1)} %get-tuple-element.9), channel_id=1, source_target_pairs={{0,448},{16,464},{32,480},{48,496},{64,0},{80,16},{96,32},{112,48}... | collective-permute-start | bytes 1966088 | tf_op jit(solution)/shard_map/ppermute | solution.py:12
  87.5 76.3 %collective-permute-start.2 = (bf16[1280,256]{0,1:T(8,128)(2,1)}, bf16[1280,256]{0,1:T(8,128)(2,1)}, u32[]{:S(2)}, u32[]{:S(2)}) collective-permute-start(bf16[1280,256]{0,1:T(8,128)(2,1)} %broadcast_select_fusion.1), channel_id=1, source_target_pairs={{0,64},{16,80},{32,96},{48,112},{64,128},{80,144},{96,160},{112,17... | collective-permute-start | bytes 1966088 | tf_op jit(solution)/shard_map/ppermute | solution.py:12
  114.3 53.4 %collective-permute-start.7 = (bf16[1280,256]{0,1:T(8,128)(2,1)}, bf16[1280,256]{0,1:T(8,128)(2,1)}, u32[]{:S(2)}, u32[]{:S(2)}) collective-permute-start(bf16[1280,256]{0,1:T(8,128)(2,1)} %fusion.17), channel_id=1, source_target_pairs={{0,384},{16,400},{32,416},{48,432},{64,448},{80,464},{96,480},{112... | collective-permute-start | bytes 1966088 | tf_op jit(solution)/shard_map/ppermute | solution.py:12
  165.8 49.9 %collective-permute-start.3 = (bf16[1280,256]{0,1:T(8,128)(2,1)}, bf16[1280,256]{0,1:T(8,128)(2,1)}, u32[]{:S(2)}, u32[]{:S(2)}) collective-permute-start(bf16[1280,256]{0,1:T(8,128)(2,1)} %broadcast_select_fusion.2), channel_id=1, source_target_pairs={{0,128},{16,144},{32,160},{48,176},{64,192},{80,208},{96,224},{112... | collective-permute-start | bytes 1966088 | tf_op jit(solution)/shard_map/ppermute | solution.py:12
  219.7 213.2 %copy-start.3 = (f32[1280]{0:T(1024)S(1)}, f32[1280]{0:T(1024)}, u32[]{:S(2)}) copy-start(f32[1280]{0:T(1024)} %param.10) | copy-start | bytes 15364
  219.7 275.9 %copy-start.2 = (f32[1280,16]{0,1:T(8,128)S(1)}, f32[1280,16]{0,1:T(8,128)}, u32[]{:S(2)}) copy-start(f32[1280,16]{0,1:T(8,128)} %param.9) | copy-start | bytes 245764
  219.7 275.9 %copy-start.4 = (f32[16]{0:T(128)S(1)}, f32[16]{0:T(128)}, u32[]{:S(2)}) copy-start(f32[16]{0:T(128)} %param.11) | copy-start | bytes 196
  495.6 64.6 %copy-start.5 = (f32[16]{0:T(128)}, f32[16]{0:T(128)S(1)}, u32[]{:S(2)}) copy-start(f32[16]{0:T(128)S(1)} %div.14) | copy-start | bytes 196
  559.5 0.7 copy-start.6
Sparse Core Ops, SparseCore 0:
  219.9 212.9 all-reduce.2
where the time goes:
time: 568 us; the launch traced here: 567 us
  waiting for transfers between devices  363 us (64%)
  blocking collectives  124 us (22%)
  starting transfers between devices  38.8 us (7%)
  between operations  15 us (3%)
  other arithmetic  14.8 us (3%)
  matrix products  7.57 us (1%)
    psum x1, waiting for transfers between devices, body(): summed = lax.psum(local_terms, 'tile')  213 us
    ppermute x8, waiting for transfers between devices, from_behind(): return lax.ppermute(value, axis, pairs)  150 us
    psum x1, blocking collectives, body(): squared = lax.psum(jnp.sum(resid * resid, axis=0), 'diag')  62.7 us
    psum x1, blocking collectives, body(): lax.psum((jnp.sum(own * hv, axis=0), jnp.sum(own * own, axis=0)), 'diag')  61.7 us
    ppermute x8, starting transfers between devices, from_behind(): return lax.ppermute(value, axis, pairs)  38.8 us
  transfers between devices with their start and end apart: 9, of which 6 were waited for; matrix products, arithmetic and copies ran while one was open for 2% of the time, Pallas kernels for 0%

commit v1 on v0

v1 whole, which is shorter than its diff:
```python
import functools

import jax
import jax.numpy as jnp
from jax import lax
from jax.experimental import pallas as pl
from jax.experimental.pallas import tpu as pltpu
from jax.sharding import PartitionSpec as P

GROUP = 128
MESH = pl.DeviceIdType.MESH
F32 = jnp.float32
BF16 = jnp.bfloat16


def tree_of(nt):
    if nt == 16:
        nodes = [(0, None), (3, 0), (-3, 0), (6, 1), (-6, 2)]
    elif nt == 4:
        nodes = [(0, None), (1, 0), (2, 1)]
    else:
        nodes = [(0, None)]
    offsets = range(-(nt // 2) + 1, nt // 2 + 1)
    sides = [[] for _ in nodes]
    for off in offsets:
        best = min(range(len(nodes)), key=lambda n: (abs(nodes[n][0] - off), n))
        sides[best].append(off)
    return nodes, sides


def kernel(
    nt, nodes, sides, rows_total,
    live_ref, vec_ref, prev_ref, energy_ref, bprev_ref, tiles_ref,
    out_ref, stat_ref,
    tile, vt, vsrc, turned, direct, tside, drecv, vch, tch, tout, row_out, rows_in,
    tile_sem, vd_send, vd_recv, vc_send, vc_recv, td_send, td_recv, tc_send, tc_recv,
    dd_send, dd_recv, st_send, st_recv,
):
    nd = 2 * nt
    size = vec_ref.shape[0]
    share = vt.shape[1]
    me_p = lax.axis_index("diag")
    me_q = lax.axis_index("tile")
    z = lax.rem(me_p, nt)
    a = lax.div(me_p, nt)
    n_nodes = len(nodes)

    load_tile = pltpu.make_async_copy(tiles_ref.at[0, 0], tile, tile_sem)
    load_tile.start()

    def plane(shift):
        return nt * a + lax.rem(z + (shift + 2 * nt), nt)

    def dest(n, off):
        home = plane(-nodes[n][0])
        q = off % nt
        return lax.rem(home + q, nd), q

    my_seg = lax.rem(me_p - me_q + nd, nd)
    my_node = jnp.int32(0)
    for n, offs in enumerate(sides):
        for off in offs:
            my_node = my_node + jnp.where(me_q == off % nt, nodes[n][0], 0)
    node_p = nt * lax.div(my_seg, nt) + lax.rem(my_seg + my_node + 2 * nt, nt)

    barrier = pltpu.get_barrier_semaphore()

    def greet(p, q):
        pl.semaphore_signal(barrier, inc=1, device_id=(p, q), device_id_type=MESH)

    expected = jnp.int32(2 * (n_nodes - 1) + (nt - 1) + (nd - 1) + 2 * nt)
    for n, (off, parent) in enumerate(nodes):
        if parent is not None:
            step = off - nodes[parent][0]
            greet(plane(step), me_q)
            greet(plane(-step), me_q)
    for n, offs in enumerate(sides):
        for off in offs:
            p, q = dest(n, off)
            if off == nodes[n][0]:
                itself = jnp.logical_and(p == me_p, q == me_q)
                expected = expected - jnp.where(itself, 2, 0)

                @pl.when(jnp.logical_not(itself))
                def _():
                    greet(p, q)
            else:
                greet(p, q)

    @pl.loop(0, nt)
    def _(j):
        @pl.when(jnp.logical_not(jnp.logical_and(node_p == me_p, j == me_q)))
        def _():
            greet(node_p, j)

    @pl.loop(1, nt)
    def _(j):
        greet(me_p, lax.rem(me_q + j, nt))

    @pl.loop(1, nd)
    def _(d):
        greet(lax.rem(me_p + d, nd), me_q)

    vt[...] = vec_ref[...].T.reshape(nt, share, size)
    pl.semaphore_wait(barrier, expected)

    def remote(src, dst, send, recv, p, q):
        return pltpu.make_async_remote_copy(
            src_ref=src, dst_ref=dst, send_sem=send, recv_sem=recv,
            device_id=(p, q), device_id_type=MESH,
        )

    def v_piece(n):
        return vt.at[me_q] if n == 0 else vch.at[n - 1]

    def v_forward(n):
        for m, (off, parent) in enumerate(nodes):
            if parent == n:
                remote(
                    v_piece(n), vch.at[m - 1], vc_send.at[m - 1], vc_recv.at[m - 1],
                    plane(off - nodes[n][0]), me_q,
                ).start()

    def v_deliver_copy(n, off):
        p, q = dest(n, off)
        return remote(
            v_piece(n), vsrc.at[me_q], vd_send.at[q], vd_recv.at[me_q], p, q
        ), jnp.logical_and(p == me_p, q == me_q)

    def v_deliver(n):
        for off in sides[n]:
            copy, itself = v_deliver_copy(n, off)
            if off == nodes[n][0]:
                @pl.when(itself)
                def _():
                    pltpu.make_async_copy(v_piece(n), vsrc.at[me_q], vd_recv.at[me_q]).start()

                @pl.when(jnp.logical_not(itself))
                def _():
                    copy.start()
            else:
                copy.start()

    def arrived(ref, sem):
        pltpu.make_async_copy(ref, ref, sem).wait()

    v_forward(0)
    v_deliver(0)

    live = live_ref[0, 0] * GROUP
    load_tile.wait()
    flat = vt[...].reshape(nt * share, size)
    lanes = lax.broadcasted_iota(jnp.int32, flat.shape, 1)
    masked = jnp.where(lanes < live, flat, jnp.zeros_like(flat))
    wide = 256 if size % 256 == 0 else 128

    @pl.loop(0, size // wide)
    def _(b):
        cols = pl.ds(pl.multiple_of(b * wide, wide), wide)
        prod = jnp.dot(masked, tile[:, cols], preferred_element_type=F32)
        turned[:, :, cols] = prod.astype(BF16).reshape(nt, share, wide)

    for n in range(1, n_nodes):
        arrived(vch.at[n - 1], vc_recv.at[n - 1])
        v_forward(n)
        v_deliver(n)

    def t_copy(j):
        return remote(
            turned.at[j], tside.at[me_q], td_send.at[j], td_recv.at[me_q], node_p, j
        ), jnp.logical_and(node_p == me_p, j == me_q)

    @pl.loop(0, nt)
    def _(i):
        j = lax.rem(i + me_q, nt)
        copy, itself = t_copy(j)

        @pl.when(itself)
        def _():
            pltpu.make_async_copy(turned.at[j], tside.at[me_q], td_recv.at[me_q]).start()

        @pl.when(jnp.logical_not(itself))
        def _():
            copy.start()

    @pl.loop(0, nt)
    def _(j):
        arrived(vsrc.at[j], vd_recv.at[j])

    source = vsrc[...].reshape(nt * share, size)

    @pl.loop(0, size // wide)
    def _(b):
        first = pl.multiple_of(b * wide, wide)
        part = pl.ds(first, wide)
        prod = lax.dot_general(
            source, tile[part, :], (((1,), (1,)), ((), ())), preferred_element_type=F32
        )
        spot = lax.broadcasted_iota(jnp.int32, prod.shape, 1) + first
        prod = jnp.where(spot < live, prod, 0.0)
        direct[:, :, part] = prod.astype(BF16).reshape(nt, share, wide)

    def d_copy(j):
        return remote(
            direct.at[j], drecv.at[me_q], dd_send.at[j], dd_recv.at[me_q], me_p, j
        )

    @pl.loop(1, nt)
    def _(i):
        d_copy(lax.rem(i + me_q, nt)).start()

    def t_up(n):
        off, parent = nodes[n]
        return remote(
            tout.at[n - 1], tch.at[n - 1], tc_send.at[n - 1], tc_recv.at[n - 1],
            plane(nodes[parent][0] - off), me_q,
        )

    total = None
    for n in reversed(range(n_nodes)):
        total = jnp.zeros((share, size), F32)
        for off in sides[n]:
            arrived(tside.at[off % nt], td_recv.at[off % nt])
            total = total + tside[off % nt].astype(F32)
        for m, (_, parent) in enumerate(nodes):
            if parent == n:
                arrived(tch.at[m - 1], tc_recv.at[m - 1])
                total = total + tch[m - 1].astype(F32)
        if n > 0:
            tout[n - 1] = total.astype(BF16)
            t_up(n).start()

    total = total + direct[me_q].astype(F32)

    def add_direct(i, acc):
        j = lax.rem(i + me_q, nt)
        arrived(drecv.at[j], dd_recv.at[j])
        return acc + drecv[j].astype(F32)

    total = lax.fori_loop(1, nt, add_direct, total)

    own = vt[me_q].astype(F32)
    hv = total + energy_ref[...] * own
    line = lax.broadcasted_iota(jnp.int32, (share, 128), 0)
    lane = lax.broadcasted_iota(jnp.int32, (share, 128), 1)

    def as_row(column, slot):
        return jnp.sum(jnp.where(lane == line + slot * share, column, 0.0), axis=0, keepdims=True)

    def as_column(row):
        return jnp.sum(jnp.where(lane == line, row, 0.0), axis=1, keepdims=True)

    w = hv - as_column(bprev_ref[...]) * prev_ref[...]
    numer = jnp.sum(own * hv, axis=1, keepdims=True)
    norm = jnp.sum(own * own, axis=1, keepdims=True)
    slope = jnp.sum(own * w, axis=1, keepdims=True) / jnp.where(norm > 0.0, norm, 1.0)
    rest = w - slope * own
    rest = jnp.sum(rest * rest, axis=1, keepdims=True)
    row_out[0] = as_row(numer, 0) + as_row(norm, 1) + as_row(slope, 2) + as_row(rest, 3)
    rows_in[me_p] = row_out[0]

    def s_copy(d):
        p = lax.rem(me_p + d, nd)
        return remote(
            row_out.at[0], rows_in.at[me_p], st_send.at[d], st_recv.at[me_p], p, me_q
        )

    @pl.loop(1, nd)
    def _(d):
        s_copy(d).start()

    @pl.loop(1, nd)
    def _(d):
        p = lax.rem(me_p + d, nd)
        arrived(rows_in.at[p], st_recv.at[p])

    rows = rows_in[...].reshape(nd, 128)
    norms = pltpu.roll(rows, 128 - share, 1)
    slopes = pltpu.roll(rows, 128 - 2 * share, 1)
    rests = pltpu.roll(rows, 128 - 3 * share, 1)
    alpha = jnp.sum(rows, axis=0, keepdims=True) / jnp.sum(norms, axis=0, keepdims=True)
    gap = slopes - alpha
    squared = jnp.sum(rests + gap * norms * gap, axis=0, keepdims=True)
    beta = jnp.sqrt(squared / rows_total + 1e-06)
    stat_ref[0:1, :] = alpha
    stat_ref[1:2, :] = beta
    out_ref[...] = (w - as_column(alpha) * own) / as_column(beta)

    for n in range(n_nodes):
        for off in sides[n]:
            copy, itself = v_deliver_copy(n, off)
            if off == nodes[n][0]:
                @pl.when(jnp.logical_not(itself))
                def _():
                    copy.wait_send()
            else:
                copy.wait_send()
        if n > 0:
            t_up(n).wait_send()
            off, parent = nodes[n]
            remote(
                v_piece(parent), vch.at[n - 1], vc_send.at[n - 1], vc_recv.at[n - 1],
                plane(off - nodes[parent][0]), me_q,
            ).wait_send()

    @pl.loop(0, nt)
    def _(j):
        copy, itself = t_copy(j)

        @pl.when(jnp.logical_not(itself))
        def _():
            copy.wait_send()

    @pl.loop(1, nt)
    def _(i):
        d_copy(lax.rem(i + me_q, nt)).wait_send()

    @pl.loop(1, nd)
    def _(d):
        s_copy(d).wait_send()


def body(tiles, live_groups, vectors, previous, energies, beta_prev):
    nt = lax.axis_size("tile")
    nd = lax.axis_size("diag")
    size, columns = vectors.shape
    share = columns // nt
    nodes, sides = tree_of(nt)
    extra = max(len(nodes) - 1, 1)
    vmem = pl.BlockSpec(memory_space=pltpu.VMEM)
    dma = pltpu.SemaphoreType.DMA
    bprev = jnp.pad(beta_prev, (0, 128 - share))[None, :]
    out, stat = pl.pallas_call(
        functools.partial(kernel, nt, nodes, sides, float(size * nd)),
        out_shape=(
            jax.ShapeDtypeStruct((share, size), F32),
            jax.ShapeDtypeStruct((2, 128), F32),
        ),
        in_specs=[
            pl.BlockSpec(memory_space=pltpu.SMEM), vmem, vmem, vmem, vmem,
            pl.BlockSpec(memory_space=pl.ANY),
        ],
        out_specs=(vmem, vmem),
        scratch_shapes=[
            pltpu.VMEM((size, size), BF16),
            pltpu.VMEM((nt, share, size), BF16),
            pltpu.VMEM((nt, share, size), BF16),
            pltpu.VMEM((nt, share, size), BF16),
            pltpu.VMEM((nt, share, size), BF16),
            pltpu.VMEM((nt, share, size), BF16),
            pltpu.VMEM((nt, share, size), BF16),
            pltpu.VMEM((extra, share, size), BF16),
            pltpu.VMEM((extra, share, size), BF16),
            pltpu.VMEM((extra, share, size), BF16),
            pltpu.VMEM((1, 1, 128), F32),
            pltpu.VMEM((nd, 1, 128), F32),
            dma, dma((nt,)), dma((nt,)), dma((extra,)), dma((extra,)),
            dma((nt,)), dma((nt,)), dma((extra,)), dma((extra,)),
            dma((nt,)), dma((nt,)), dma((nd,)), dma((nd,)),
        ],
        compiler_params=pltpu.CompilerParams(
            collective_id=0, has_side_effects=True, vmem_limit_bytes=40 * 1024 * 1024
        ),
    )(live_groups, vectors, previous.T, energies[None, :], bprev, tiles)
    return out.T, stat[0, :share], stat[1, :share]


def solution(mesh):
    return jax.shard_map(
        body,
        mesh=mesh,
        in_specs=(
            P("diag", "tile", None, None),
            P("diag", "tile"),
            P("diag", None),
            P("diag", "tile"),
            P("diag"),
            P("tile"),
        ),
        out_specs=(P("diag", "tile"), P("tile"), P("tile")),
        check_vma=False,
    )
```

time: 568 us -> 77.7 us (0.14)
  the two profiles are of different devices: /device:TPU:32 before, /device:TPU:12 now
where the time goes in v1:
time: 77.7 us; the launch traced here: 77.4 us
  Pallas kernels  69.7 us (90%)
  local copies, waits for them, and re-layouts  6.41 us (8%)
  between operations  1.29 us (2%)
    pallas_call x1, Pallas kernels, body(): pl.pallas_call(functools.partial(kernel, nt, nodes, sides, float(size * n...  69.7 us
    unnamed x7, local copies, waits for them, and re-layouts  4.53 us

profile of v1, /device:TPU:12, one launch (start us, length us, event | category | flops | bytes accessed | tf_op | source)
XLA Modules:
  0.0 77.4 jit_solution(3016559063115199650)
XLA Ops:
  1.3 0.7 pad_bitcast_fusion.bprev_ref
  1.9 0.7 broadcast_in_dim.6.energy_ref
  2.6 0.0 copy-start
  2.6 1.9 %copy-done = bf16[1,1,1280,1280]{3,2,1,0:T(8,128)(2,1)S(1)} copy-done((bf16[1,1,1280,1280]{3,2,1,0:T(8,128)(2,1)S(1)}, bf16[1,1,1280,1280]{3,2,1,0:T(8,128)(2,1)}, u32[]{:S(2)}) %copy-start) | copy-done | bytes 3276824
  4.6 0.0 copy-start.1
  4.6 1.1 %copy-done.1 = bf16[1280,256]{1,0:T(8,128)(2,1)S(1)} copy-done((bf16[1280,256]{1,0:T(8,128)(2,1)S(1)}, bf16[1280,256]{1,0:T(8,128)(2,1)}, u32[]{:S(2)}) %copy-start.1) | copy-done | bytes 655384
  5.7 0.0 copy-start.2
  5.7 0.9 %copy-done.2 = f32[1280,16]{0,1:T(8,128)S(1)} copy-done((f32[1280,16]{0,1:T(8,128)S(1)}, f32[1280,16]{0,1:T(8,128)}, u32[]{:S(2)}) %copy-start.2) | copy-done | bytes 81944
  6.5 69.7 %shard_map.85 = (f32[16,1280]{1,0:T(8,128)S(1)}, f32[2,128]{1,0:T(2,128)S(1)}) custom-call(s32[1,1]{1,0:T(1,128)S(6)} %copy.10.live_ref, bf16[1280,256]{1,0:T(8,128)(2,1)S(1)} %copy-done.1, f32[16,1280]{1,0:T(8,128)S(1)} %bitcast.9, f32[1,1280]{1,0:T(1,128)S(1)} %broadcast_in_dim.6.energy_ref, f32[1,128]{1,0:T(1,128)S(1)} %pad_bitcast_fusion.bprev_ref, ...), custom_call_target="tpu_custom_call" | custom-call | tf_op jit(solution)/shard_map/pallas_call | solution.py:333
  76.2 0.5 slice_bitcast_fusion
  76.7 0.6 copy.11
Async XLA Ops:
  2.6 1.9 %copy-start = (bf16[1,1,1280,1280]{3,2,1,0:T(8,128)(2,1)S(1)}, bf16[1,1,1280,1280]{3,2,1,0:T(8,128)(2,1)}, u32[]{:S(2)}) copy-start(bf16[1,1,1280,1280]{3,2,1,0:T(8,128)(2,1)} %tiles_ref.1) | copy-start | bytes 9830404
  4.6 1.1 %copy-start.1 = (bf16[1280,256]{1,0:T(8,128)(2,1)S(1)}, bf16[1280,256]{1,0:T(8,128)(2,1)}, u32[]{:S(2)}) copy-start(bf16[1280,256]{1,0:T(8,128)(2,1)} %vec_ref.1) | copy-start | bytes 1966084
  5.7 0.9 %copy-start.2 = (f32[1280,16]{0,1:T(8,128)S(1)}, f32[1280,16]{0,1:T(8,128)}, u32[]{:S(2)}) copy-start(f32[1280,16]{0,1:T(8,128)} %param.9) | copy-start | bytes 245764

commit v2 on v0

v2 whole, which is shorter than its diff:
```python
import functools

import jax
import jax.numpy as jnp
from jax import lax
from jax.experimental import pallas as pl
from jax.experimental.pallas import tpu as pltpu
from jax.sharding import PartitionSpec as P

GROUP = 128
MESH = pl.DeviceIdType.MESH
F32 = jnp.float32
BF16 = jnp.bfloat16
ORDER = ((1, 0), (3, 0), (0, 1), (2, 0), (1, 1), (3, 1), (2, 1))
VMEM_MIB = 58
PLAN = (('v', 0), ('product', 0), ('t', 6), ('v', 1), ('v', 2), ('t', 4), ('turn', 0), ('v', 3), ('v', 4), ('t', 6), ('node', 5), ('node', 3), ('node', 4), ('d', 0), ('d', 1), ('share', 0), ('node', 1), ('node', 2))
SMALL = (("v", 0), ("product", 0), ("t", 2), ("v", 1), ("turn", 0), ("v", 2), ("t", 2), ("node", 1), ("d", 0), ("d", 1), ("node", 2), ("share", 0))


def offsets_of(nt):
    return range(-(nt // 2) + 1, nt // 2 + 1)


def tree_of(nt, nodes):
    sides = [[] for _ in nodes]
    for off in offsets_of(nt):
        best = min(range(len(nodes)), key=lambda n: (abs(nodes[n][0] - off), n))
        sides[best].append(off)
    return nodes, sides


def trees_of(nt):
    if nt == 16:
        chain = [(0, None), (3, 0), (-3, 0), (6, 1), (-6, 2)]
        return tree_of(nt, chain), tree_of(nt, chain + [(8, 0)])
    if nt == 4:
        return tree_of(nt, [(0, None), (1, 0), (2, 1)]), tree_of(nt, [(0, None), (1, 0), (-1, 0)])
    return tree_of(nt, [(0, None)]), tree_of(nt, [(0, None)])


def kernel(
    nt, v_tree, t_tree, rows_total,
    live_ref, energy_ref, bprev_ref, vec_ref, prev_ref, tiles_ref,
    out_ref, alpha_ref, beta_ref,
    vec, prev, tile, flipped, vt, vsrc, turned, tside, dpart, dxch, dsend, drecv, vch, tch, tout,
    row_out, rows_in,
    vec_sem, prev_sem, tile_sem,
    vd_send, vd_recv, vc_send, vc_recv, td_send, td_recv, tc_send, tc_recv,
    dx_send, dx_recv, dd_send, dd_recv, s_send, s_recv,
):
    nd = 2 * nt
    ny = nt // 4
    size = vec_ref.shape[0]
    share = vt.shape[1]
    me_p = lax.axis_index("diag")
    me_q = lax.axis_index("tile")
    z = lax.rem(me_p, nt)
    a = lax.div(me_p, nt)
    core = lax.rem(me_q, 2)
    chip = lax.div(me_q, 2)
    across = lax.rem(chip, 2)
    y = lax.div(chip, 2)
    v_nodes, v_sides = v_tree
    t_nodes, t_sides = t_tree

    load_vec = pltpu.make_async_copy(vec_ref, vec, vec_sem)
    load_vec.start()
    load_tile = pltpu.make_async_copy(tiles_ref.at[0, 0], tile, tile_sem)
    load_tile.start()
    load_prev = pltpu.make_async_copy(prev_ref, prev, prev_sem)
    load_prev.start()

    def plane(shift):
        return nt * a + lax.rem(z + (shift + 2 * nt), nt)

    def dest(nodes, n, off):
        home = plane(-nodes[n][0])
        q = lax.rem(off + nt, nt)
        p = lax.rem(home + q, nd)
        return p, q, jnp.logical_and(p == me_p, q == me_q)

    my_seg = lax.rem(me_p - me_q + nd, nd)

    def node_plane(nodes, sides):
        shift = jnp.int32(0)
        for n, offs in enumerate(sides):
            for off in offs:
                shift = shift + jnp.where(me_q == off % nt, nodes[n][0], 0)
        return nt * lax.div(my_seg, nt) + lax.rem(my_seg + shift + 2 * nt, nt)

    v_from = node_plane(v_nodes, v_sides)
    t_to = node_plane(t_nodes, t_sides)

    def chip_at(dy, db):
        row = lax.rem(y + dy + (ny - 2 * dy) * core + ny, ny)
        return 2 * row + lax.rem(across + db, 2)

    moves = [(dy, db) for dy, db in ORDER if dy < ny]
    spots = [(dy, db, dc) for dc in range(2) for dy, db in moves + [(0, 0)]]

    def tile_at(dy, db, dc):
        return 2 * chip_at(dy, db) + lax.rem(core + dc, 2)

    shifts = sorted(range(1, nt), key=lambda d: -min(d, nt - d)) + [0]
    others = [(da, dz) for dz in shifts for da in (1, 0) if (da, dz) != (0, 0)]

    def segment(da, dz):
        return nt * lax.rem(a + da, 2) + lax.rem(z + dz, nt)

    barrier = pltpu.get_barrier_semaphore()

    def greet(p, q):
        pl.semaphore_signal(barrier, inc=1, device_id=(p, q), device_id_type=MESH)

    expected = jnp.int32(0)

    def greet_unless(p, q, itself):
        @pl.when(jnp.logical_not(itself))
        def _():
            greet(p, q)

        return jnp.where(itself, 0, 1)

    def greet_tree(nodes, sides, home, v):
        count = jnp.int32(0)
        for n, (off, parent) in enumerate(nodes):
            if parent is not None:
                step = off - nodes[parent][0]
                greet(plane(step), me_q)
                greet(plane(-step), me_q)
                count = count + 2
        for n, offs in enumerate(sides):
            for off in offs:
                count = count + greet_unless(*dest(nodes, n, off))
        for j in range(nt):
            count = count + greet_unless(home, j, jnp.logical_and(home == me_p, j == me_q))
        return count

    expected = expected + greet_tree(v_nodes, v_sides, v_from, True)
    expected = expected + greet_tree(t_nodes, t_sides, t_to, False)
    greet(me_p, me_q + 1 - 2 * core)
    for dy, db in moves:
        greet(me_p, 2 * chip_at(dy, db) + core)
    for da, dz in others:
        greet(segment(da, dz), me_q)
    expected = expected + (1 + len(moves) + len(others))

    load_vec.wait()
    vt[...] = vec[...].T.reshape(nt, share, size)
    pl.semaphore_wait(barrier, expected)

    def remote(src, dst, send, recv, p, q):
        return pltpu.make_async_remote_copy(
            src_ref=src, dst_ref=dst, send_sem=send, recv_sem=recv,
            device_id=(p, q), device_id_type=MESH,
        )

    def arrived(ref, sem):
        pltpu.make_async_copy(ref, ref, sem).wait()

    def v_piece(n):
        return vt.at[me_q] if n == 0 else vch.at[n - 1]

    def v_hop(m):
        off, parent = v_nodes[m]
        return remote(
            v_piece(parent), vch.at[m - 1], vc_send.at[m - 1], vc_recv.at[m - 1],
            plane(off - v_nodes[parent][0]), me_q,
        )

    def v_forward(n):
        for m, (_, parent) in enumerate(v_nodes):
            if parent == n:
                v_hop(m).start()

    def v_out(n, off):
        p, q, itself = dest(v_nodes, n, off)
        return remote(v_piece(n), vsrc.at[me_q], vd_send.at[q], vd_recv.at[me_q], p, q), itself

    def v_deliver(n):
        count = len(v_sides[n])
        for i in range(count):
            off = v_sides[n][0] + lax.rem(me_q + i, count)
            copy, itself = v_out(n, off)

            @pl.when(itself)
            def _():
                pltpu.make_async_copy(v_piece(n), vsrc.at[me_q], vd_recv.at[me_q]).start()

            @pl.when(jnp.logical_not(itself))
            def _():
                copy.start()

    live = live_ref[0, 0] * GROUP
    wide = 256 if size % 256 == 0 else 128

    def v_stage(n):
        if n > 0:
            arrived(vch.at[n - 1], vc_recv.at[n - 1])
        v_forward(n)
        v_deliver(n)

    def t_product():
        flat = vt[...].reshape(nt * share, size)
        lanes = lax.broadcasted_iota(jnp.int32, flat.shape, 1)
        masked = jnp.where(lanes < live, flat, jnp.zeros_like(flat))
        load_tile.wait()

        @pl.loop(0, size // wide)
        def _(b):
            cols = pl.ds(pl.multiple_of(b * wide, wide), wide)
            prod = jnp.dot(masked, tile[:, cols], preferred_element_type=F32)
            turned[:, :, cols] = prod.astype(BF16).reshape(nt, share, wide)

    def t_turn():
        @pl.loop(0, size // wide)
        def _(b):
            first = pl.multiple_of(b * wide, wide)
            part = pl.ds(first, wide)
            block = tile[part, :].T
            spot = lax.broadcasted_iota(jnp.int32, block.shape, 1) + first
            flipped[:, part] = jnp.where(spot < live, block, jnp.zeros_like(block))

    def t_out(j):
        return remote(
            turned.at[j], tside.at[me_q], td_send.at[j], td_recv.at[me_q], t_to, j
        ), jnp.logical_and(t_to == me_p, j == me_q)

    def t_send(group):
        for spot in group:
            j = tile_at(*spot)
            copy, itself = t_out(j)

            @pl.when(itself)
            def _():
                pltpu.make_async_copy(turned.at[j], tside.at[me_q], td_recv.at[me_q]).start()

            @pl.when(jnp.logical_not(itself))
            def _():
                copy.start()

    def t_up(n):
        off, parent = t_nodes[n]
        return remote(
            tout.at[n - 1], tch.at[n - 1], tc_send.at[n - 1], tc_recv.at[n - 1],
            plane(t_nodes[parent][0] - off), me_q,
        )

    def t_sum(n):
        total = jnp.zeros((share, size), F32)
        for off in t_sides[n]:
            arrived(tside.at[off % nt], td_recv.at[off % nt])
            total = total + tside[off % nt].astype(F32)
        for m, (_, parent) in enumerate(t_nodes):
            if parent == n:
                arrived(tch.at[m - 1], tc_recv.at[m - 1])
                total = total + tch[m - 1].astype(F32)
        return total

    def t_node(n):
        tout[n - 1] = t_sum(n).astype(BF16)
        t_up(n).start()

    half = nt * share // 2
    m_half = nt // 4

    def d_product(h):
        for j in range(h * nt // 2, (h + 1) * nt // 2):
            arrived(vsrc.at[j], vd_recv.at[j])
        source = vsrc[pl.ds(h * nt // 2, nt // 2)].reshape(half, size)

        @pl.loop(0, size // wide)
        def _(b):
            part = pl.ds(pl.multiple_of(b * wide, wide), wide)
            prod = jnp.dot(source, flipped[:, part], preferred_element_type=F32)
            prod = prod.reshape(m_half, 2, share, wide)
            dpart[0, pl.ds(h * m_half, m_half), :, part] = prod[:, 0]
            dpart[1, pl.ds(h * m_half, m_half), :, part] = prod[:, 1]

        d_swap(h).start()

    def d_swap(h):
        part = pl.ds(h * m_half, m_half)
        return remote(
            dpart.at[1 - core, part], dxch.at[part], dx_send.at[h], dx_recv.at[h],
            me_p, me_q + 1 - 2 * core,
        )

    def d_out(dy, db):
        m = chip_at(dy, db)
        return remote(
            dsend.at[m], drecv.at[chip], dd_send.at[m], dd_recv.at[chip], me_p, 2 * m + core
        ), m

    def d_share():
        for h in range(2):
            arrived(dxch.at[pl.ds(h * m_half, m_half)], dx_recv.at[h])
        for dy, db in moves:
            copy, m = d_out(dy, db)
            dsend[m] = (dpart[core, m] + dxch[m]).astype(BF16)
            copy.start()

    at = 0
    for word, number in PLAN if nt == 16 else SMALL:
        if word == "v":
            v_stage(number)
        elif word == "product":
            t_product()
        elif word == "turn":
            t_turn()
        elif word == "t":
            t_send(spots[at : at + number])
            at += number
        elif word == "node":
            t_node(number)
        elif word == "d":
            d_product(number)
        elif word == "share":
            d_share()

    total = t_sum(0) + dpart[core, chip] + dxch[chip]
    for dy, db in moves:
        m = chip_at(dy, db)
        arrived(drecv.at[m], dd_recv.at[m])
        total = total + drecv[m].astype(F32)

    own = vt[me_q].astype(F32)
    hv = total + energy_ref[...].reshape(1, size) * own
    line = lax.broadcasted_iota(jnp.int32, (share, 128), 0)
    lane = lax.broadcasted_iota(jnp.int32, (share, 128), 1)

    def as_row(column, slot):
        return jnp.sum(jnp.where(lane == line + slot * share, column, 0.0), axis=0, keepdims=True)

    def as_column(row):
        return jnp.sum(jnp.where(lane == line, row, 0.0), axis=1, keepdims=True)

    load_prev.wait()
    square = [lax.broadcasted_iota(jnp.int32, (share, share), d) for d in range(2)]
    before = jnp.where(square[0] == square[1], bprev_ref[...].reshape(1, share), 0.0)
    before = jnp.sum(before, axis=1, keepdims=True)
    w = hv - before * prev[...]
    numer = jnp.sum(own * hv, axis=1, keepdims=True)
    norm = jnp.sum(own * own, axis=1, keepdims=True)
    slope = jnp.sum(own * w, axis=1, keepdims=True) / jnp.where(norm > 0.0, norm, 1.0)
    rest = w - slope * own
    rest = jnp.sum(rest * rest, axis=1, keepdims=True)
    row_out[0] = as_row(numer, 0) + as_row(norm, 1) + as_row(slope, 2) + as_row(rest, 3)
    for da, dz in others:
        remote(row_out.at[0], rows_in.at[me_p], s_send, s_recv, segment(da, dz), me_q).start()
    rows_in[me_p] = row_out[0]
    arrived(rows_in.at[pl.ds(0, nd - 1)], s_recv)

    rows = rows_in[...].reshape(nd, 128)
    norms = pltpu.roll(rows, 128 - share, 1)
    slopes = pltpu.roll(rows, 128 - 2 * share, 1)
    rests = pltpu.roll(rows, 128 - 3 * share, 1)
    alpha = jnp.sum(rows, axis=0, keepdims=True) / jnp.sum(norms, axis=0, keepdims=True)
    gap = slopes - alpha
    squared = jnp.sum(rests + gap * norms * gap, axis=0, keepdims=True)
    beta = jnp.sqrt(squared / rows_total + 1e-06)
    alpha_ref[...] = alpha
    beta_ref[...] = beta
    out_ref[...] = (w - as_column(alpha) * own) / as_column(beta)

    for n in range(len(v_nodes)):
        for off in v_sides[n]:
            copy, itself = v_out(n, off)

            @pl.when(jnp.logical_not(itself))
            def _():
                copy.wait_send()

        if n > 0:
            v_hop(n).wait_send()
    for n in range(1, len(t_nodes)):
        t_up(n).wait_send()
    for j in range(nt):
        copy, itself = t_out(j)

        @pl.when(jnp.logical_not(itself))
        def _():
            copy.wait_send()

    for h in range(2):
        d_swap(h).wait_send()
    for dy, db in moves:
        d_out(dy, db)[0].wait_send()
    arrived(rows_in.at[pl.ds(0, nd - 1)], s_send)


def body(tiles, live_groups, vectors, previous, energies, beta_prev):
    nt = lax.axis_size("tile")
    nd = lax.axis_size("diag")
    size, columns = vectors.shape
    share = columns // nt
    v_tree, t_tree = trees_of(nt)
    v_more, t_more = max(len(v_tree[0]) - 1, 1), max(len(t_tree[0]) - 1, 1)
    vmem = pl.BlockSpec(memory_space=pltpu.VMEM)
    hbm = pl.BlockSpec(memory_space=pl.ANY)
    dma = pltpu.SemaphoreType.DMA
    out, alpha, beta = pl.pallas_call(
        functools.partial(kernel, nt, v_tree, t_tree, float(size * nd)),
        out_shape=(
            jax.ShapeDtypeStruct((share, size), F32),
            jax.ShapeDtypeStruct((1, 128), F32),
            jax.ShapeDtypeStruct((1, 128), F32),
        ),
        in_specs=[pl.BlockSpec(memory_space=pltpu.SMEM), vmem, vmem, hbm, hbm, hbm],
        out_specs=(vmem, vmem, vmem),
        scratch_shapes=[
            pltpu.VMEM((size, columns), BF16),
            pltpu.VMEM((share, size), F32),
            pltpu.VMEM((size, size), BF16),
            pltpu.VMEM((size, size), BF16),
            pltpu.VMEM((nt, share, size), BF16),
            pltpu.VMEM((nt, share, size), BF16),
            pltpu.VMEM((nt, share, size), BF16),
            pltpu.VMEM((nt, share, size), BF16),
            pltpu.VMEM((2, nt // 2, share, size), F32),
            pltpu.VMEM((nt // 2, share, size), F32),
            pltpu.VMEM((nt // 2, share, size), BF16),
            pltpu.VMEM((nt // 2, share, size), BF16),
            pltpu.VMEM((v_more, share, size), BF16),
            pltpu.VMEM((t_more, share, size), BF16),
            pltpu.VMEM((t_more, share, size), BF16),
            pltpu.VMEM((1, 1, 128), F32),
            pltpu.VMEM((nd, 1, 128), F32),
            dma, dma, dma,
            dma((nt,)), dma((nt,)), dma((v_more,)), dma((v_more,)),
            dma((nt,)), dma((nt,)), dma((t_more,)), dma((t_more,)),
            dma((2,)), dma((2,)), dma((nt // 2,)), dma((nt // 2,)),
            dma, dma,
        ],
        compiler_params=pltpu.CompilerParams(
            collective_id=0, has_side_effects=True, vmem_limit_bytes=VMEM_MIB * 1024 * 1024
        ),
    )(live_groups, energies, beta_prev, vectors, previous.T, tiles)
    return out.T, alpha[0, :share], beta[0, :share]


def solution(mesh):
    return jax.shard_map(
        body,
        mesh=mesh,
        in_specs=(
            P("diag", "tile", None, None),
            P("diag", "tile"),
            P("diag", None),
            P("diag", "tile"),
            P("diag"),
            P("tile"),
        ),
        out_specs=(P("diag", "tile"), P("tile"), P("tile")),
        check_vma=False,
    )
```

time: 568 us -> 64.8 us (0.11)
  the two profiles are of different devices: /device:TPU:32 before, /device:TPU:2 now
where the time goes in v2:
time: 64.8 us; the launch traced here: 64.6 us
  Pallas kernels  60.6 us (94%)
  local copies, waits for them, and re-layouts  2.73 us (4%)
  between operations  1.29 us (2%)
    pallas_call x1, Pallas kernels, body(): pl.pallas_call(functools.partial(kernel, nt, v_tree, t_tree, float(size *...  60.6 us
    unnamed x1, local copies, waits for them, and re-layouts  1.53 us

profile of v2, /device:TPU:2, one launch (start us, length us, event | category | flops | bytes accessed | tf_op | source)
XLA Modules:
  0.0 64.6 jit_solution(5581301678943690727)
XLA Ops:
  1.3 60.6 %shard_map.85 = (f32[16,1280]{1,0:T(8,128)}, f32[1,128]{1,0:T(1,128)}, f32[1,128]{1,0:T(1,128)}) custom-call(s32[1,1]{1,0:T(1,128)S(6)} %copy.10.live_ref, f32[1280]{0:T(1024)} %energy_ref.1, f32[16]{0:T(128)} %bprev_ref.1, bf16[1280,256]{1,0:T(8,128)(2,1)} %vec_ref.1, f32[16,1280]{1,0:T(8,128)} %bitcast.7, bf16[1,1,1280,1280]{3,2,1,0:T(8,128)(2,1)} %tiles_ref.1), custom_call_target="tpu_custom_call" | custom-call | tf_op jit(solution)/shard_map/pallas_call | solution.py:402
  61.9 1.2 %slice_bitcast_fusion = (f32[16]{0:T(128)}, f32[16]{0:T(128)}) fusion(f32[1,128]{1,0:T(1,128)} %get-tuple-element.8, f32[1,128]{1,0:T(1,128)} %get-tuple-element.7), kind=kLoop, calls=%fused_computation | loop fusion | bytes 256 | tf_op jit(solution)/shard_map/squeeze | solution.py:439
  63.1 1.5 %copy.11 = f32[1280,16]{0,1:T(8,128)} copy(f32[1280,16]{0,1:T(8,128)} %bitcast.6) | data formatting | bytes 163840

commit v3 on v2

v3 whole, which is shorter than its diff:
```python
import functools

import jax
import jax.numpy as jnp
from jax import lax
from jax.experimental import pallas as pl
from jax.experimental.pallas import tpu as pltpu
from jax.sharding import PartitionSpec as P

GROUP = 128
MESH = pl.DeviceIdType.MESH
F32 = jnp.float32
BF16 = jnp.bfloat16
ORDER = ((1, 0), (3, 0), (0, 1), (2, 0), (1, 1), (3, 1), (2, 1))
VMEM_MIB = 58
FAR = 3
V_PARTS = 2
T_PARTS = 2
PLAN = (('product', 0), ('greeted', 0), ('v', 0), ('far', 8), ('mid', 8), ('near', 4), ('turn', 0), ('v', 1), ('v', 2), ('far', 8), ('mid', 8), ('v', 3), ('v', 4), ('near', 12), ('node', 5), ('node', 3), ('node', 4), ('d', 0), ('d', 1), ('share', 0), ('node', 1), ('node', 2))
SMALL = (("greeted", 0), ("v", 0), ("product", 0), ("near", 2), ("v", 1), ("turn", 0), ("v", 2), ("near", 2), ("node", 2), ("node", 1), ("d", 0), ("d", 1), ("share", 0))


def offsets_of(nt):
    return range(-(nt // 2) + 1, nt // 2 + 1)


def tree_of(nt, nodes):
    sides = [[] for _ in nodes]
    for off in offsets_of(nt):
        best = min(range(len(nodes)), key=lambda n: (abs(nodes[n][0] - off), n))
        sides[best].append(off)
    return nodes, sides


def trees_of(nt):
    if nt == 16:
        chain = [(0, None), (3, 0), (-3, 0), (6, 1), (-6, 2)]
        return tree_of(nt, chain), tree_of(nt, chain + [(8, FAR)])
    if nt == 4:
        return tree_of(nt, [(0, None), (1, 0), (2, 1)]), tree_of(nt, [(0, None), (1, 0), (2, 1)])
    return tree_of(nt, [(0, None)]), tree_of(nt, [(0, None)])


def kernel(
    nt, v_tree, t_tree, rows_total,
    live_in, energy_in, bprev_in, vec_ref, prev_ref, tiles_ref,
    out_ref, alpha_ref, beta_ref,
    live_ref, energy_ref, bprev_ref, vec, prev, tile, flipped, other, vt, vsrc, turned, tside, dpart, dsend, drecv, vch, tch, tout,
    row_out, rows_in,
    live_sem, energy_sem, bprev_sem, vec_sem, prev_sem, tile_sem,
    vd_send, vd_recv, vc_send, vc_recv, td_send, td_recv, tc_send, tc_recv,
    f_send, f_recv, dd_send, dd_recv, s_send, s_recv,
):
    nd = 2 * nt
    ny = nt // 4
    size = vec_ref.shape[0]
    share = vt.shape[1]
    me_p = lax.axis_index("diag")
    me_q = lax.axis_index("tile")
    z = lax.rem(me_p, nt)
    a = lax.div(me_p, nt)
    core = lax.rem(me_q, 2)
    chip = lax.div(me_q, 2)
    across = lax.rem(chip, 2)
    y = lax.div(chip, 2)
    v_nodes, v_sides = v_tree
    t_nodes, t_sides = t_tree

    load_vec = pltpu.make_async_copy(vec_ref, vec, vec_sem)
    load_vec.start()
    load_tile = pltpu.make_async_copy(tiles_ref.at[0, 0], tile, tile_sem)
    load_tile.start()
    load_prev = pltpu.make_async_copy(prev_ref, prev, prev_sem)
    load_prev.start()
    load_live = pltpu.make_async_copy(live_in, live_ref, live_sem)
    load_live.start()
    load_energy = pltpu.make_async_copy(energy_in, energy_ref, energy_sem)
    load_energy.start()
    load_bprev = pltpu.make_async_copy(bprev_in, bprev_ref, bprev_sem)
    load_bprev.start()

    def plane(shift):
        return nt * a + lax.rem(z + (shift + 2 * nt), nt)

    def dest(nodes, n, off):
        home = plane(-nodes[n][0])
        q = lax.rem(off + nt, nt)
        return lax.rem(home + q, nd), q

    def v_dest(n, off):
        p, q = dest(v_nodes, n, off)
        to = 2 * lax.div(q, 2) + core
        return p, q, to, jnp.logical_and(p == me_p, to == me_q)

    def node_plane(nodes, sides, q):
        seg = lax.rem(me_p - q + nd, nd)
        shift = jnp.int32(0)
        for n, offs in enumerate(sides):
            for off in offs:
                shift = shift + jnp.where(q == off % nt, nodes[n][0], 0)
        return nt * lax.div(seg, nt) + lax.rem(seg + shift + 2 * nt, nt)

    t_to = node_plane(t_nodes, t_sides, me_q)

    def chip_at(dy, db):
        row = lax.rem(y + dy + (ny - 2 * dy) * core + ny, ny)
        return 2 * row + lax.rem(across + db, 2)

    moves = [(dy, db) for dy, db in ORDER if dy < ny]
    spots = [(dy, db, dc) for dc in range(2) for dy, db in moves + [(0, 0)]]

    def tile_at(dy, db, dc):
        return 2 * chip_at(dy, db) + lax.rem(core + dc, 2)

    shifts = sorted(range(1, nt), key=lambda d: -min(d, nt - d)) + [0]
    others = [(da, dz) for dz in shifts for da in (1, 0) if (da, dz) != (0, 0)]

    def segment(da, dz):
        return nt * lax.rem(a + da, 2) + lax.rem(z + dz, nt)

    barrier = pltpu.get_barrier_semaphore()

    def greet(p, q):
        pl.semaphore_signal(barrier, inc=1, device_id=(p, q), device_id_type=MESH)

    expected = jnp.int32(0)

    def greet_unless(p, q, itself):
        @pl.when(jnp.logical_not(itself))
        def _():
            greet(p, q)

        return jnp.where(itself, 0, 1)

    def greet_chain(nodes):
        for off, parent in nodes:
            if parent is not None:
                step = off - nodes[parent][0]
                greet(plane(step), me_q)
                greet(plane(-step), me_q)
        return 2 * (len(nodes) - 1)

    expected = expected + greet_chain(v_nodes) + greet_chain(t_nodes)
    for n, offs in enumerate(v_sides):
        for off in offs:
            p, _, to, itself = v_dest(n, off)
            expected = expected + greet_unless(p, to, itself)
    for e in range(2):
        home = node_plane(v_nodes, v_sides, 2 * chip + e)
        for m in range(nt // 2):
            itself = jnp.logical_and(home == me_p, chip == m)
            expected = expected + greet_unless(home, 2 * m + core, itself)
    for n, offs in enumerate(t_sides):
        for off in offs:
            p, q = dest(t_nodes, n, off)
            itself = jnp.logical_and(p == me_p, q == me_q)
            expected = expected + greet_unless(p, q, itself)
    for j in range(nt):
        itself = jnp.logical_and(t_to == me_p, j == me_q)
        expected = expected + greet_unless(t_to, j, itself)
    for j in range(1, nt):
        greet(me_p, lax.rem(me_q + j, nt))
    greet(lax.rem(me_p + nt, nd), me_q)
    expected = expected + nt

    load_vec.wait()
    vt[...] = vec[...].T.reshape(nt, share, size)

    def remote(src, dst, send, recv, p, q):
        return pltpu.make_async_remote_copy(
            src_ref=src, dst_ref=dst, send_sem=send, recv_sem=recv,
            device_id=(p, q), device_id_type=MESH,
        )

    def arrived(ref, sem):
        pltpu.make_async_copy(ref, ref, sem).wait()

    v_cut, t_cut = ([pl.ds(i * size // n, size // n) for i in range(n)] for n in (V_PARTS, T_PARTS))

    def v_piece(n):
        return vt.at[me_q] if n == 0 else vch.at[n - 1]

    def v_hop(m, i):
        off, parent = v_nodes[m]
        return remote(
            v_piece(parent).at[:, v_cut[i]], vch.at[m - 1, :, v_cut[i]],
            vc_send.at[m - 1, i], vc_recv.at[m - 1, i],
            plane(off - v_nodes[parent][0]), me_q,
        )

    def v_forward(n, i):
        for m, (_, parent) in enumerate(v_nodes):
            if parent == n:
                v_hop(m, i).start()

    def v_out(n, off):
        p, q, to, itself = v_dest(n, off)
        e = lax.rem(q, 2)
        return (
            remote(v_piece(n), vsrc.at[e, chip], vd_send.at[q], vd_recv.at[e, chip], p, to),
            pltpu.make_async_copy(v_piece(n), vsrc.at[e, chip], vd_recv.at[e, chip]),
            itself,
        )

    def v_deliver(n):
        count = len(v_sides[n])
        for i in range(count):
            off = v_sides[n][0] + lax.rem(me_q + i, count)
            copy, stay, itself = v_out(n, off)

            @pl.when(itself)
            def _():
                stay.start()

            @pl.when(jnp.logical_not(itself))
            def _():
                copy.start()

    load_live.wait()
    live = live_ref[0, 0] * GROUP
    wide = 256 if size % 256 == 0 else 128

    def v_stage(n):
        for i, part in enumerate(v_cut):
            if n > 0:
                arrived(vch.at[n - 1, :, part], vc_recv.at[n - 1, i])
            v_forward(n, i)

    def t_product():
        flat = vt[...].reshape(nt * share, size)
        lanes = lax.broadcasted_iota(jnp.int32, flat.shape, 1)
        masked = jnp.where(lanes < live, flat, jnp.zeros_like(flat))
        load_tile.wait()

        @pl.loop(0, size // wide)
        def _(b):
            cols = pl.ds(pl.multiple_of(b * wide, wide), wide)
            prod = jnp.dot(masked, tile[:, cols], preferred_element_type=F32)
            turned[:, :, cols] = prod.astype(BF16).reshape(nt, share, wide)

    def f_swap():
        return remote(flipped, other, f_send, f_recv, me_p, me_q + 1 - 2 * core)

    def t_turn():
        @pl.loop(0, size // wide)
        def _(b):
            first = pl.multiple_of(b * wide, wide)
            part = pl.ds(first, wide)
            block = tile[part, :].T
            spot = lax.broadcasted_iota(jnp.int32, block.shape, 1) + first
            flipped[:, part] = jnp.where(spot < live, block, jnp.zeros_like(block))

        f_swap().start()

    def t_out(j):
        return remote(
            turned.at[j], tside.at[me_q], td_send.at[j], td_recv.at[me_q], t_to, j
        ), jnp.logical_and(t_to == me_p, j == me_q)

    def t_send(group):
        for spot in group:
            j = tile_at(*spot)
            copy, itself = t_out(j)

            @pl.when(itself)
            def _():
                pltpu.make_async_copy(turned.at[j], tside.at[me_q], td_recv.at[me_q]).start()

            @pl.when(jnp.logical_not(itself))
            def _():
                copy.start()

    def t_up(n, i):
        off, parent = t_nodes[n]
        return remote(
            tout.at[n - 1, :, t_cut[i]], tch.at[n - 1, :, t_cut[i]],
            tc_send.at[n - 1, i], tc_recv.at[n - 1, i],
            plane(t_nodes[parent][0] - off), me_q,
        )

    def t_sum(n, i):
        part = t_cut[i]
        total = None
        for off in t_sides[n]:
            if i == 0:
                arrived(tside.at[off % nt], td_recv.at[off % nt])
            piece = tside[off % nt, :, part].astype(F32)
            total = piece if total is None else total + piece
        for m, (_, parent) in enumerate(t_nodes):
            if parent == n:
                arrived(tch.at[m - 1, :, part], tc_recv.at[m - 1, i])
                total = total + tch[m - 1, :, part].astype(F32)
        return total

    def t_node(n):
        for i in range(T_PARTS):
            tout[n - 1, :, t_cut[i]] = t_sum(n, i).astype(BF16)
            t_up(n, i).start()

    half = nt * share // 2

    def d_product(second):
        e = 1 - core if second else core
        for m in range(nt // 2):
            arrived(vsrc.at[e, m], vd_recv.at[e, m])
        if second:
            arrived(other, f_recv)
        source = vsrc[e].reshape(half, size)

        @pl.loop(0, size // wide)
        def _(b):
            part = pl.ds(pl.multiple_of(b * wide, wide), wide)
            block = other[:, part] if second else flipped[:, part]
            prod = jnp.dot(source, block, preferred_element_type=F32).reshape(-1, share, wide)
            if second:
                prod = prod + dpart[:, :, part]
                dsend[:, :, part] = prod.astype(BF16)
            dpart[:, :, part] = prod

    def d_out(dy, db):
        m = chip_at(dy, db)
        return remote(
            dsend.at[m], drecv.at[chip], dd_send.at[m], dd_recv.at[chip], me_p, 2 * m + core
        ), m

    def d_share():
        for dy, db in moves:
            d_out(dy, db)[0].start()

    rank = jnp.int32(0)
    for n, offs in enumerate(t_sides):
        for off in offs:
            rank = rank + jnp.where(me_q == off % nt, min(abs(t_nodes[n][0]) // 3, 2), 0)
    at = [0, 0, 0]
    for word, number in PLAN if nt == 16 else SMALL:
        if word == "v":
            v_stage(number)
            v_deliver(number)
        elif word == "vf":
            v_stage(number)
        elif word == "vd":
            v_deliver(number)
        elif word == "greeted":
            pl.semaphore_wait(barrier, expected)
        elif word == "product":
            t_product()
        elif word == "turn":
            t_turn()
        elif word in ("near", "mid", "far"):
            k = ("near", "mid", "far").index(word)
            sent, at[k] = spots[at[k] : at[k] + number], at[k] + number

            @pl.when(rank == k)
            def _():
                t_send(sent)
        elif word == "node":
            t_node(number)
        elif word == "d":
            d_product(number)
        elif word == "share":
            d_share()

    line = lax.broadcasted_iota(jnp.int32, (share, 128), 0)
    lane = lax.broadcasted_iota(jnp.int32, (share, 128), 1)

    def as_row(column, slot):
        return jnp.sum(jnp.where(lane == line + slot * share, column, 0.0), axis=0, keepdims=True)

    def as_column(row):
        return jnp.sum(jnp.where(lane == line, row, 0.0), axis=1, keepdims=True)

    load_energy.wait()
    load_bprev.wait()
    load_prev.wait()
    square = [lax.broadcasted_iota(jnp.int32, (share, share), d) for d in range(2)]
    before = jnp.where(square[0] == square[1], bprev_ref[...].reshape(1, share), 0.0)
    before = jnp.sum(before, axis=1, keepdims=True)
    own = vt[me_q].astype(F32)
    diagonal = energy_ref[...].reshape(1, size) * own
    behind = before * prev[...]
    norm = jnp.sum(own * own, axis=1, keepdims=True)
    back = jnp.sum(own * behind, axis=1, keepdims=True)

    total = jnp.concatenate([t_sum(0, i) for i in range(T_PARTS)], axis=1)
    total = total + dpart[chip]
    for dy, db in moves:
        m = chip_at(dy, db)
        arrived(drecv.at[m], dd_recv.at[m])
        total = total + drecv[m].astype(F32)

    hv = total + diagonal
    w = hv - behind
    numer = jnp.sum(own * hv, axis=1, keepdims=True)
    slope = (numer - back) / jnp.where(norm > 0.0, norm, 1.0)
    rest = w - slope * own
    rest = jnp.sum(rest * rest, axis=1, keepdims=True)
    row_out[0] = as_row(numer, 0) + as_row(norm, 1) + as_row(slope, 2) + as_row(rest, 3)
    for da, dz in others:
        remote(row_out.at[0], rows_in.at[me_p], s_send, s_recv, segment(da, dz), me_q).start()
    rows_in[me_p] = row_out[0]
    arrived(rows_in.at[pl.ds(0, nd - 1)], s_recv)

    rows = rows_in[...].reshape(nd, 128)
    norms = pltpu.roll(rows, 128 - share, 1)
    slopes = pltpu.roll(rows, 128 - 2 * share, 1)
    rests = pltpu.roll(rows, 128 - 3 * share, 1)
    alpha = jnp.sum(rows, axis=0, keepdims=True) / jnp.sum(norms, axis=0, keepdims=True)
    gap = slopes - alpha
    squared = jnp.sum(rests + gap * norms * gap, axis=0, keepdims=True)
    beta = jnp.sqrt(squared / rows_total + 1e-06)
    alpha_ref[...] = alpha
    beta_ref[...] = beta
    out_ref[...] = (w - as_column(alpha) * own) / as_column(beta)

    for n in range(len(v_nodes)):
        for off in v_sides[n]:
            copy, _, itself = v_out(n, off)

            @pl.when(jnp.logical_not(itself))
            def _():
                copy.wait_send()

        if n > 0:
            for i in range(V_PARTS):
                v_hop(n, i).wait_send()
    for n in range(1, len(t_nodes)):
        for i in range(T_PARTS):
            t_up(n, i).wait_send()
    for j in range(nt):
        copy, itself = t_out(j)

        @pl.when(jnp.logical_not(itself))
        def _():
            copy.wait_send()

    f_swap().wait_send()
    for dy, db in moves:
        d_out(dy, db)[0].wait_send()
    arrived(rows_in.at[pl.ds(0, nd - 1)], s_send)


def body(tiles, live_groups, vectors, previous, energies, beta_prev):
    nt = lax.axis_size("tile")
    nd = lax.axis_size("diag")
    size, columns = vectors.shape
    share = columns // nt
    v_tree, t_tree = trees_of(nt)
    v_more, t_more = max(len(v_tree[0]) - 1, 1), max(len(t_tree[0]) - 1, 1)
    vmem = pl.BlockSpec(memory_space=pltpu.VMEM)
    hbm = pl.BlockSpec(memory_space=pl.ANY)
    dma = pltpu.SemaphoreType.DMA
    out, alpha, beta = pl.pallas_call(
        functools.partial(kernel, nt, v_tree, t_tree, float(size * nd)),
        out_shape=(
            jax.ShapeDtypeStruct((share, size), F32),
            jax.ShapeDtypeStruct((1, 128), F32),
            jax.ShapeDtypeStruct((1, 128), F32),
        ),
        in_specs=[hbm] * 6,
        out_specs=(vmem, vmem, vmem),
        scratch_shapes=[
            pltpu.SMEM((1, 1), jnp.int32),
            pltpu.VMEM((size,), F32),
            pltpu.VMEM((share,), F32),
            pltpu.VMEM((size, columns), BF16),
            pltpu.VMEM((share, size), F32),
            pltpu.VMEM((size, size), BF16),
            pltpu.VMEM((size, size), BF16),
            pltpu.VMEM((size, size), BF16),
            pltpu.VMEM((nt, share, size), BF16),
            pltpu.VMEM((2, nt // 2, share, size), BF16),
            pltpu.VMEM((nt, share, size), BF16),
            pltpu.VMEM((nt, share, size), BF16),
            pltpu.VMEM((nt // 2, share, size), F32),
            pltpu.VMEM((nt // 2, share, size), BF16),
            pltpu.VMEM((nt // 2, share, size), BF16),
            pltpu.VMEM((v_more, share, size), BF16),
            pltpu.VMEM((t_more, share, size), BF16),
            pltpu.VMEM((t_more, share, size), BF16),
            pltpu.VMEM((1, 1, 128), F32),
            pltpu.VMEM((nd, 1, 128), F32),
            dma, dma, dma, dma, dma, dma,
            dma((nt,)), dma((2, nt // 2)), dma((v_more, V_PARTS)), dma((v_more, V_PARTS)),
            dma((nt,)), dma((nt,)), dma((t_more, T_PARTS)), dma((t_more, T_PARTS)),
            dma, dma, dma((nt // 2,)), dma((nt // 2,)),
            dma, dma,
        ],
        compiler_params=pltpu.CompilerParams(
            collective_id=0, has_side_effects=True, vmem_limit_bytes=VMEM_MIB * 1024 * 1024
        ),
    )(live_groups, energies, beta_prev, vectors, previous.T, tiles)
    return out.T, alpha[0, :share], beta[0, :share]


def solution(mesh):
    return jax.shard_map(
        body,
        mesh=mesh,
        in_specs=(
            P("diag", "tile", None, None),
            P("diag", "tile"),
            P("diag", None),
            P("diag", "tile"),
            P("diag"),
            P("tile"),
        ),
        out_specs=(P("diag", "tile"), P("tile"), P("tile")),
        check_vma=False,
    )
```

time: 64.8 us -> 61.7 us (0.952)
  Pallas kernels: 60.6 us -> 57.6 us
    pallas_call x1, Pallas kernels: 60.6 us -> 57.6 us  [body(): pl.pallas_call(functools.partial(kernel, nt, v_tree, t_tree, float(size *...]
where the time goes in v3:
time: 61.7 us; the launch traced here: 61.6 us
  Pallas kernels  57.6 us (93%)
  local copies, waits for them, and re-layouts  2.73 us (4%)
  between operations  1.29 us (2%)
    pallas_call x1, Pallas kernels, body(): pl.pallas_call(functools.partial(kernel, nt, v_tree, t_tree, float(size *...  57.6 us
    unnamed x1, local copies, waits for them, and re-layouts  1.53 us

profile of v3, /device:TPU:2, one launch (start us, length us, event | category | flops | bytes accessed | tf_op | source)
XLA Modules:
  0.0 61.6 jit_solution(18176367475079375909)
XLA Ops:
  1.3 57.6 %shard_map.85 = (f32[16,1280]{1,0:T(8,128)}, f32[1,128]{1,0:T(1,128)}, f32[1,128]{1,0:T(1,128)}) custom-call(s32[1,1]{1,0:T(1,128)S(6)} %copy.10.live_in, f32[1280]{0:T(1024)} %energy_in.1, f32[16]{0:T(128)} %bprev_in.1, bf16[1280,256]{1,0:T(8,128)(2,1)} %vec_ref.1, f32[16,1280]{1,0:T(8,128)} %bitcast.7, bf16[1,1,1280,1280]{3,2,1,0:T(8,128)(2,1)} %tiles_ref.1), custom_call_target="tpu_custom_call" | custom-call | tf_op jit(solution)/shard_map/pallas_call | solution.py:452
  58.8 1.2 %slice_bitcast_fusion = (f32[16]{0:T(128)}, f32[16]{0:T(128)}) fusion(f32[1,128]{1,0:T(1,128)} %get-tuple-element.8, f32[1,128]{1,0:T(1,128)} %get-tuple-element.7), kind=kLoop, calls=%fused_computation | loop fusion | bytes 256 | tf_op jit(solution)/shard_map/squeeze | solution.py:492
  60.0 1.5 %copy.11 = f32[1280,16]{0,1:T(8,128)} copy(f32[1280,16]{0,1:T(8,128)} %bitcast.6) | data formatting | bytes 163840

commit v4 on v3

--- a/solution.py
+++ b/solution.py
@@ -13,10 +13,9 @@
 BF16 = jnp.bfloat16
 ORDER = ((1, 0), (3, 0), (0, 1), (2, 0), (1, 1), (3, 1), (2, 1))
 VMEM_MIB = 58
-FAR = 3
-V_PARTS = 2
-T_PARTS = 2
-PLAN = (('product', 0), ('greeted', 0), ('v', 0), ('far', 8), ('mid', 8), ('near', 4), ('turn', 0), ('v', 1), ('v', 2), ('far', 8), ('mid', 8), ('v', 3), ('v', 4), ('near', 12), ('node', 5), ('node', 3), ('node', 4), ('d', 0), ('d', 1), ('share', 0), ('node', 1), ('node', 2))
+V_PARTS = 1
+T_PARTS = 1
+PLAN = (('product', 0), ('greeted', 0), ('v', 0), ('far', 8), ('mid', 8), ('near', 8), ('turn', 0), ('v', 1), ('v', 2), ('far', 8), ('mid', 8), ('near', 8), ('v', 3), ('v', 4), ('node', 5), ('node', 3), ('node', 4), ('d', 0), ('d', 1), ('node', 1), ('node', 2))
 SMALL = (("greeted", 0), ("v", 0), ("product", 0), ("near", 2), ("v", 1), ("turn", 0), ("v", 2), ("near", 2), ("node", 2), ("node", 1), ("d", 0), ("d", 1), ("share", 0))
 
 
@@ -35,7 +34,7 @@
 def trees_of(nt):
     if nt == 16:
         chain = [(0, None), (3, 0), (-3, 0), (6, 1), (-6, 2)]
-        return tree_of(nt, chain), tree_of(nt, chain + [(8, FAR)])
+        return tree_of(nt, chain), tree_of(nt, chain + [(8, 3)])
     if nt == 4:
         return tree_of(nt, [(0, None), (1, 0), (2, 1)]), tree_of(nt, [(0, None), (1, 0), (2, 1)])
     return tree_of(nt, [(0, None)]), tree_of(nt, [(0, None)])
@@ -103,7 +102,7 @@
     t_to = node_plane(t_nodes, t_sides, me_q)
 
     def chip_at(dy, db):
-        row = lax.rem(y + dy + (ny - 2 * dy) * core + ny, ny)
+        row = lax.rem(y + dy, ny)
         return 2 * row + lax.rem(across + db, 2)
 
     moves = [(dy, db) for dy, db in ORDER if dy < ny]
@@ -297,6 +296,23 @@
             tout[n - 1, :, t_cut[i]] = t_sum(n, i).astype(BF16)
             t_up(n, i).start()
 
+    blocks = size // wide
+    d_cut = [(0, blocks - blocks // 2), (blocks - blocks // 2, blocks)][: min(blocks, 2)]
+
+    def d_part(i):
+        return pl.ds(d_cut[i][0] * wide, (d_cut[i][1] - d_cut[i][0]) * wide)
+
+    def d_out(dy, db, i):
+        m = chip_at(dy, db)
+        return remote(
+            dsend.at[m, :, d_part(i)], drecv.at[chip, :, d_part(i)],
+            dd_send.at[m, i], dd_recv.at[chip, i], me_p, 2 * m + core,
+        )
+
+    def d_share(i):
+        for dy, db in moves:
+            d_out(dy, db, i).start()
+
     half = nt * share // 2
 
     def d_product(second):
@@ -307,8 +323,7 @@
             arrived(other, f_recv)
         source = vsrc[e].reshape(half, size)
 
-        @pl.loop(0, size // wide)
-        def _(b):
+        def columns(b):
             part = pl.ds(pl.multiple_of(b * wide, wide), wide)
             block = other[:, part] if second else flipped[:, part]
             prod = jnp.dot(source, block, preferred_element_type=F32).reshape(-1, share, wide)
@@ -317,15 +332,12 @@
                 dsend[:, :, part] = prod.astype(BF16)
             dpart[:, :, part] = prod
 
-    def d_out(dy, db):
-        m = chip_at(dy, db)
-        return remote(
-            dsend.at[m], drecv.at[chip], dd_send.at[m], dd_recv.at[chip], me_p, 2 * m + core
-        ), m
-
-    def d_share():
-        for dy, db in moves:
-            d_out(dy, db)[0].start()
+        if second:
+            for i, (first, last) in enumerate(d_cut):
+                pl.loop(first, last)(columns)
+                d_share(i)
+        else:
+            pl.loop(0, size // wide)(columns)
 
     rank = jnp.int32(0)
     for n, offs in enumerate(t_sides):
@@ -357,8 +369,6 @@
             t_node(number)
         elif word == "d":
             d_product(number)
-        elif word == "share":
-            d_share()
 
     line = lax.broadcasted_iota(jnp.int32, (share, 128), 0)
     lane = lax.broadcasted_iota(jnp.int32, (share, 128), 1)
@@ -385,7 +395,8 @@
     total = total + dpart[chip]
     for dy, db in moves:
         m = chip_at(dy, db)
-        arrived(drecv.at[m], dd_recv.at[m])
+        for i in range(len(d_cut)):
+            arrived(drecv.at[m, :, d_part(i)], dd_recv.at[m, i])
         total = total + drecv[m].astype(F32)
 
     hv = total + diagonal
@@ -435,7 +446,8 @@
 
     f_swap().wait_send()
     for dy, db in moves:
-        d_out(dy, db)[0].wait_send()
+        for i in range(len(d_cut)):
+            d_out(dy, db, i).wait_send()
     arrived(rows_in.at[pl.ds(0, nd - 1)], s_send)
 
 
@@ -482,7 +494,7 @@
             dma, dma, dma, dma, dma, dma,
             dma((nt,)), dma((2, nt // 2)), dma((v_more, V_PARTS)), dma((v_more, V_PARTS)),
             dma((nt,)), dma((nt,)), dma((t_more, T_PARTS)), dma((t_more, T_PARTS)),
-            dma, dma, dma((nt // 2,)), dma((nt // 2,)),
+            dma, dma, dma((nt // 2, 2)), dma((nt // 2, 2)),
             dma, dma,
         ],
         compiler_params=pltpu.CompilerParams(

time: 61.7 us -> 61.1 us (level)
  Pallas kernels: 57.6 us -> 56.9 us
    pallas_call x1, Pallas kernels: 57.6 us -> 56.9 us  [body(): pl.pallas_call(functools.partial(kernel, nt, v_tree, t_tree, float(size *...]
where the time goes in v4:
time: 61.1 us; the launch traced here: 60.9 us
  Pallas kernels  56.9 us (93%)
  local copies, waits for them, and re-layouts  2.73 us (4%)
  between operations  1.29 us (2%)
    pallas_call x1, Pallas kernels, body(): pl.pallas_call(functools.partial(kernel, nt, v_tree, t_tree, float(size *...  56.9 us
    unnamed x1, local copies, waits for them, and re-layouts  1.53 us

profile of v4, /device:TPU:2, one launch (start us, length us, event | category | flops | bytes accessed | tf_op | source)
XLA Modules:
  0.0 60.9 jit_solution(14865474375996835476)
XLA Ops:
  1.3 56.9 %shard_map.85 = (f32[16,1280]{1,0:T(8,128)}, f32[1,128]{1,0:T(1,128)}, f32[1,128]{1,0:T(1,128)}) custom-call(s32[1,1]{1,0:T(1,128)S(6)} %copy.10.live_in, f32[1280]{0:T(1024)} %energy_in.1, f32[16]{0:T(128)} %bprev_in.1, bf16[1280,256]{1,0:T(8,128)(2,1)} %vec_ref.1, f32[16,1280]{1,0:T(8,128)} %bitcast.7, bf16[1,1,1280,1280]{3,2,1,0:T(8,128)(2,1)} %tiles_ref.1), custom_call_target="tpu_custom_call" | custom-call | tf_op jit(solution)/shard_map/pallas_call | solution.py:464
  58.2 1.2 %slice_bitcast_fusion = (f32[16]{0:T(128)}, f32[16]{0:T(128)}) fusion(f32[1,128]{1,0:T(1,128)} %get-tuple-element.8, f32[1,128]{1,0:T(1,128)} %get-tuple-element.7), kind=kLoop, calls=%fused_computation | loop fusion | bytes 256 | tf_op jit(solution)/shard_map/squeeze | solution.py:504
  59.4 1.5 %copy.11 = f32[1280,16]{0,1:T(8,128)} copy(f32[1280,16]{0,1:T(8,128)} %bitcast.6) | data formatting | bytes 163840

commit v5 on v4

--- a/solution.py
+++ b/solution.py
@@ -11,10 +11,10 @@
 MESH = pl.DeviceIdType.MESH
 F32 = jnp.float32
 BF16 = jnp.bfloat16
-ORDER = ((1, 0), (3, 0), (0, 1), (2, 0), (1, 1), (3, 1), (2, 1))
-VMEM_MIB = 58
+ORDER = ((1, 0), (3, 0), (0, 1), (1, 1), (3, 1), (2, 0), (2, 1))
+VMEM_KIB = 54784
 V_PARTS = 1
-T_PARTS = 1
+T_PARTS = 2
 PLAN = (('product', 0), ('greeted', 0), ('v', 0), ('far', 8), ('mid', 8), ('near', 8), ('turn', 0), ('v', 1), ('v', 2), ('far', 8), ('mid', 8), ('near', 8), ('v', 3), ('v', 4), ('node', 5), ('node', 3), ('node', 4), ('d', 0), ('d', 1), ('node', 1), ('node', 2))
 SMALL = (("greeted", 0), ("v", 0), ("product", 0), ("near", 2), ("v", 1), ("turn", 0), ("v", 2), ("near", 2), ("node", 2), ("node", 1), ("d", 0), ("d", 1), ("share", 0))
 
@@ -498,7 +498,7 @@
             dma, dma,
         ],
         compiler_params=pltpu.CompilerParams(
-            collective_id=0, has_side_effects=True, vmem_limit_bytes=VMEM_MIB * 1024 * 1024
+            collective_id=0, has_side_effects=True, vmem_limit_bytes=VMEM_KIB * 1024
         ),
     )(live_groups, energies, beta_prev, vectors, previous.T, tiles)
     return out.T, alpha[0, :share], beta[0, :share]

time: 61.1 us -> 61.2 us (level)
  local copies, waits for them, and re-layouts: 2.73 us -> 3.38 us
    unnamed x1 -> x7, local copies, waits for them, and re-layouts: 1.53 us -> 2.87 us
    squeeze x1, local copies, waits for them, and re-layouts: 1.2 us -> 0.52 us  [body(): return (out.T, alpha[0, :share], beta[0, :share])]
    pallas_call x1, Pallas kernels: 56.9 us -> 56.3 us  [body(): pl.pallas_call(functools.partial(kernel, nt, v_tree, t_tree, float(size *...]
where the time goes in v5:
time: 61.2 us; the launch traced here: 61 us
  Pallas kernels  56.3 us (92%)
  local copies, waits for them, and re-layouts  3.38 us (6%)
  between operations  1.3 us (2%)
    pallas_call x1, Pallas kernels, body(): pl.pallas_call(functools.partial(kernel, nt, v_tree, t_tree, float(size *...  56.3 us
    unnamed x7, local copies, waits for them, and re-layouts  2.87 us

profile of v5, /device:TPU:2, one launch (start us, length us, event | category | flops | bytes accessed | tf_op | source)
XLA Modules:
  0.0 61.0 jit_solution(14303601619707642301)
XLA Ops:
  1.3 0.0 copy-start
  1.3 0.9 %copy-done = f32[1280,16]{0,1:T(8,128)S(1)} copy-done((f32[1280,16]{0,1:T(8,128)S(1)}, f32[1280,16]{0,1:T(8,128)}, u32[]{:S(2)}) %copy-start) | copy-done | bytes 81944
  2.2 0.0 copy-start.1
  2.2 0.7 %copy-done.1 = f32[1280]{0:T(1024)S(1)} copy-done((f32[1280]{0:T(1024)S(1)}, f32[1280]{0:T(1024)}, u32[]{:S(2)}) %copy-start.1) | copy-done | bytes 5144
  2.9 0.0 copy-start.2
  2.9 0.7 %copy-done.2 = f32[16]{0:T(128)S(1)} copy-done((f32[16]{0:T(128)S(1)}, f32[16]{0:T(128)}, u32[]{:S(2)}) %copy-start.2) | copy-done | bytes 88
  3.5 56.3 %shard_map.85 = (f32[16,1280]{1,0:T(8,128)S(1)}, f32[1,128]{1,0:T(1,128)S(1)}, f32[1,128]{1,0:T(1,128)S(1)}) custom-call(s32[1,1]{1,0:T(1,128)S(6)} %copy.10.live_in, f32[1280]{0:T(1024)S(1)} %copy-done.1, f32[16]{0:T(128)S(1)} %copy-done.2, bf16[1280,256]{1,0:T(8,128)(2,1)} %vec_ref.1, f32[16,1280]{1,0:T(8,128)S(1)} %bitcast.7, ...), custom_call_target="tpu_custom_call" | custom-call | tf_op jit(solution)/shard_map/pallas_call | solution.py:464
  59.8 0.5 slice_bitcast_fusion
  60.3 0.6 %copy.11 = f32[1280,16]{0,1:T(8,128)} copy(f32[1280,16]{0,1:T(8,128)S(1)} %bitcast.6) | data formatting | bytes 163840
Async XLA Ops:
  1.3 0.9 %copy-start = (f32[1280,16]{0,1:T(8,128)S(1)}, f32[1280,16]{0,1:T(8,128)}, u32[]{:S(2)}) copy-start(f32[1280,16]{0,1:T(8,128)} %param.9) | copy-start | bytes 245764
  2.2 0.7 %copy-start.1 = (f32[1280]{0:T(1024)S(1)}, f32[1280]{0:T(1024)}, u32[]{:S(2)}) copy-start(f32[1280]{0:T(1024)} %energy_in.1) | copy-start | bytes 15364
  2.9 0.7 %copy-start.2 = (f32[16]{0:T(128)S(1)}, f32[16]{0:T(128)}, u32[]{:S(2)}) copy-start(f32[16]{0:T(128)} %bprev_in.1) | copy-start | bytes 196
